TPU v7x, 32 devices: a whole 2x2x4 slice. The times are simulated.
32 devices in a mesh: layer: 2 (over core), dict: 16 (over z, y, x).
Axes of the slice: x: 2, y: 2, z: 4, core: 2. Of those that a mesh axis runs over, the one named last changes fastest.
Arguments:
- hidden: bfloat16 [2, 512, 9216], P('layer', None, 'dict'), may hold values from -6 to 6
- row_list: int32 [512], replicated, may hold values from 0 to 511, each once
- w_down: bfloat16 [2, 9216, 2304], P('layer', 'dict'), may hold values from -0.0625 to 0.0625
- w_enc: bfloat16 [2, 2304, 8192], P('layer', None, 'dict'), may hold values from -0.09375 to 0.09375
- b_enc: float32 [8192], P('dict'), may hold values from -3 to 3
- w_dec: float32 [2, 8192, 2304], P('layer', 'dict'), may hold values from -0.0625 to 0.0625
- b_dec: float32 [2, 2304], P('layer'), may hold values from -3 to 3
- alive_mask: int32 [8192], P('dict'), may hold values 0 or 1
Outputs:
- latent: bfloat16 [512, 8192], P('layer', 'dict')
- residual: float32 [2, 512, 2304], P('layer', 'dict')
- adjoint: float32 [512, 8192], P('layer', 'dict')
Inputs may be any that keep to these rules, and one draw needn't show every extreme that they name: `row_list`: a permutation of the 512 buffer rows.
All inputs are finite; a program needn't handle non-finite values. No bound on the sum of `alive_mask` on one device may be relied on, other than what follows from the above.
Results may differ from a plain program's by a relative error of at most 0.0045.
Values may be sent and summed in bfloat16 or wider, within the bound.
A program may use at most 64 MiB of HBM per device.

v0:
```python
import jax
import jax.numpy as jnp
from jax import lax
from jax.sharding import PartitionSpec as P


def per_device(hidden, row_list, w_down, w_enc, b_enc, w_dec, b_dec, alive_mask):
    chosen = jnp.take(hidden, row_list, axis=1)
    row_count = chosen.shape[1]
    dict_count = lax.axis_size("dict")
    share_rows = row_count // dict_count
    layer_rows = row_count // lax.axis_size("layer")
    dict_start = lax.axis_index("dict") * share_rows
    layer_start = lax.axis_index("layer") * layer_rows
    alive_float = alive_mask.astype(jnp.float32)
    partial_value = jnp.einsum("krf,kfd->rkd", chosen, w_down, preferred_element_type=jnp.float32)
    activations = lax.psum(partial_value, "dict").astype(jnp.bfloat16)
    encoded = jnp.einsum("rkd,kdl->rl", activations, w_enc, preferred_element_type=jnp.float32)
    preact = lax.psum(encoded, "layer") + b_enc
    latent = (jnp.maximum(preact, 0.0) * alive_float).astype(jnp.bfloat16)
    latent_wide = latent.astype(jnp.float32)
    terms = jnp.einsum(
        "rl,kld->rkd",
        latent_wide,
        w_dec,
        precision=lax.Precision.HIGHEST,
        preferred_element_type=jnp.float32,
    )
    rebuilt = lax.psum(terms, "dict")
    remainder = activations.astype(jnp.float32) - (rebuilt + b_dec)
    residual_own = lax.dynamic_slice_in_dim(remainder, dict_start, share_rows, 0)
    adjoint = (
        lax.psum_scatter(
            -jnp.einsum(
                "rkd,kld->rl",
                remainder,
                w_dec,
                precision=lax.Precision.HIGHEST,
                preferred_element_type=jnp.float32,
            ),
            "layer",
            scatter_dimension=0,
            tiled=True,
        )
        * alive_float
    )
    latent_own = lax.dynamic_slice_in_dim(latent, layer_start, layer_rows, 0)
    residual_out = jnp.transpose(residual_own, (1, 0, 2))
    return (latent_own, residual_out, adjoint)


def solution(mesh):
    return jax.shard_map(
        per_device,
        mesh=mesh,
        in_specs=(
            P("layer", None, "dict"),
            P(),
            P("layer", "dict", None),
            P("layer", None, "dict"),
            P("dict"),
            P("layer", "dict", None),
            P("layer", None),
            P("dict"),
        ),
        out_specs=(P("layer", "dict"), P("layer", "dict", None), P("layer", "dict")),
        check_vma=False,
    )
```

profile of v0, /device:TPU:1, one launch (start us, length us, event | category | flops | bytes accessed | tf_op | source)
XLA Modules:
  0.0 473.2 jit_solution(3164656298936381022)
XLA Ops:
  7.2 0.0 all-reduce.4.cloned.1.call-start
  7.2 0.8 compare_select_fusion
  8.1 0.7 compare_and_fusion
  8.8 1.4 copy.11
  10.1 2.7 gather_fusion
  12.8 5.3 %convolution_bitcast_fusion.1 = f32[512,1,2304]{2,0,1:T(8,128)} fusion(bf16[1,576,2304]{2,1,0:T(8,128)(2,1)S(1)} %copy-done, bf16[512,576]{1,0:T(8,128)(2,1)} %gather_fusion, pred[512]{0:T(512)(128)(4,1)S(1)} %compare_and_fusion), kind=kOutput, calls=%fused_computation.2 | convolution fusion | flops 1359249408 | bytes 7963136 | tf_op jit(solution)/shard_map/krf,kfd->rkd/dot_general | solution.py:16
  18.1 208.7 %all-reduce.7 = bf16[512,1,2304]{2,0,1:T(8,128)(2,1)} all-reduce(f32[512,1,2304]{2,0,1:T(8,128)} %convolution_bitcast_fusion.1), channel_id=1, replica_groups=mesh['layer'=2,'dict'=16] {'dict'}, use_global_device_ids=true, to_apply=%region_0.1 | all-reduce | flops 1179648 | bytes 7077888 | tf_op jit(solution)/shard_map/psum | solution.py:17
  226.8 4.8 %fusion.5 = f32[512,512]{1,0:T(8,128)} fusion(bf16[1,2304,512]{2,1,0:T(8,128)(2,1)} %param.11, bf16[512,1,2304]{2,0,1:T(8,128)(2,1)} %all-reduce.7), kind=kOutput, calls=%fused_computation.9 | convolution fusion | flops 1207959552 | bytes 5767168 | tf_op jit(solution)/shard_map/rkd,kdl->rl/dot_general | solution.py:18
  231.6 0.0 all-reduce.4.cloned.1.call-update
  231.7 0.0 all-reduce.6.cloned.1.call-start
  231.7 18.0 %all-reduce.4.cloned.1.call-done = f32[512,512]{1,0:T(8,128)} async-done(((f32[512,512]{1,0:T(8,128)}), f32[512,512]{1,0:T(8,128)}) %all-reduce.4.cloned.1.call-update) | async-done | bytes 1048592 | tf_op jit(solution)/shard_map/psum | solution.py:19
  249.7 1.4 multiply_convert_fusion
  251.1 8.9 %convolution_bitcast_fusion = f32[512,1,2304]{2,0,1:T(8,128)} fusion(bf16[512,512]{1,0:T(8,128)(2,1)S(1)} %multiply_convert_fusion, f32[1,512,2304]{2,1,0:T(8,128)} %param.13), kind=kOutput, calls=%fused_computation.1 | convolution fusion | flops 7247757312 | bytes 9961472 | tf_op jit(solution)/shard_map/rl,kld->rkd/dot_general | solution.py:22
  260.0 0.0 all-reduce.6.cloned.1.call-update
  260.0 0.0 reduce-scatter.2.cloned.1.call-start
  260.1 0.6 copy-done.2
  260.7 179.9 %all-reduce.6.cloned.1.call-done = f32[512,1,2304]{2,0,1:T(8,128)} async-done(((f32[512,1,2304]{2,0,1:T(8,128)}), f32[512,1,2304]{2,0,1:T(8,128)}) %all-reduce.6.cloned.1.call-update) | async-done | bytes 4718608 | tf_op jit(solution)/shard_map/psum | solution.py:29
  440.6 3.6 add_subtract_fusion
  444.2 2.1 copy-done.1
  446.3 10.3 %fusion.8 = f32[512,512]{1,0:T(8,128)} fusion(f32[1,512,2304]{2,1,0:T(8,128)} %param.13, f32[512,1,2304]{2,0,1:T(8,128)S(1)} %add_subtract_fusion), kind=kOutput, calls=%fused_computation.12 | convolution fusion | flops 7248019456 | bytes 10485760 | tf_op jit(solution)/shard_map/rkd,kld->rl/dot_general | solution.py:34
  456.6 0.7 constant_dynamic-slice_fusion
  457.3 1.7 dynamic-slice_bitcast_fusion
  459.0 5.7 %reduce-scatter.2.cloned.1.call-done = f32[256,512]{1,0:T(8,128)} async-done(((f32[512,512]{1,0:T(8,128)}), f32[256,512]{1,0:T(8,128)}) %reduce-scatter.2.cloned.1.call-update) | async-done | bytes 524304 | tf_op jit(solution)/shard_map/reduce_scatter | solution.py:33
  464.7 1.9 broadcast_multiply_fusion
  (12 shorter events, 0.1 us)
Async XLA Ops:
  7.2 5.7 %copy-start = (bf16[1,576,2304]{2,1,0:T(8,128)(2,1)S(1)}, bf16[1,576,2304]{2,1,0:T(8,128)(2,1)}, u32[]{:S(2)}) copy-start(bf16[1,576,2304]{2,1,0:T(8,128)(2,1)} %param.10) | copy-start | bytes 7962628
  7.2 242.6 %all-reduce.4.cloned.1.call-start = ((), (), s32[]{:S(2)}) async-start(), calls=%async_computation.1 | async-start | bytes 2097152 | tf_op jit(solution)/shard_map/psum | solution.py:19
  226.8 4.9 %copy-start.4 = (s32[512]{0:T(512)S(1)}, s32[512]{0:T(512)}, u32[]{:S(2)}) copy-start(s32[512]{0:T(512)} %param.15) | copy-start | bytes 6148
  226.8 22.9 %copy-start.3 = (f32[512]{0:T(512)S(1)}, f32[512]{0:T(512)}, u32[]{:S(2)}) copy-start(f32[512]{0:T(512)} %param.12) | copy-start | bytes 6148
  231.7 208.9 %all-reduce.6.cloned.1.call-start = ((), (), s32[]{:S(2)}) async-start(), calls=%async_computation.2 | async-start | bytes 9437184 | tf_op jit(solution)/shard_map/psum | solution.py:29
  260.0 0.7 copy-start.2
  260.0 204.7 %reduce-scatter.2.cloned.1.call-start = ((), (), s32[]{:S(2)}) async-start(), calls=%async_computation.3 | async-start | bytes 1572864 | tf_op jit(solution)/shard_map/reduce_scatter | solution.py:33
  444.2 2.1 copy-start.1
Sparse Core Ops, SparseCore 0:
  231.8 17.9 all-reduce.3
  260.1 180.4 all-reduce.5
  456.7 7.9 reduce-scatter.1
where the time goes:
time: 474 us; the launch traced here: 473 us
  blocking collectives  209 us (44%)
  waiting for transfers between devices  204 us (43%)
  matrix products  29.3 us (6%)
  between operations  13.8 us (3%)
  local copies, waits for them, and re-layouts  9.23 us (2%)
  other arithmetic  8.38 us (2%)
    psum x1, blocking collectives, per_device(): activations = lax.psum(partial_value, 'dict').astype(jnp.bfloat16)  209 us
    psum x1, waiting for transfers between devices, per_device(): rebuilt = lax.psum(terms, 'dict')  180 us
    psum x1, waiting for transfers between devices, per_device(): preact = lax.psum(encoded, 'layer') + b_enc  18 us
    dot_general x1, matrix products, per_device(): jnp.einsum('rkd,kld->rl', remainder, w_dec, precision=lax.Precision.HIGHE...  10.3 us
  transfers between devices with their start and end apart: 3, of which 3 were waited for; matrix products, arithmetic and copies ran while one was open for 1% of the time, Pallas kernels for 0%

commit v1 on v0

v1 whole, which is shorter than its diff:
```python
import functools
import math

import jax
import jax.numpy as jnp
from jax import lax
from jax.experimental import pallas as pl
from jax.experimental.pallas import tpu as pltpu
from jax.sharding import PartitionSpec as P

F32, BF16, I32 = jnp.float32, jnp.bfloat16, jnp.int32
PARTS = 2


def digits_of(mesh):
    line = list(mesh.devices.reshape(mesh.shape["layer"], -1)[0])
    count = len(line)
    try:
        coords = [tuple(d.coords) for d in line]
    except (AttributeError, TypeError):
        coords = None
    sizes = []
    if coords:
        found = []
        for axis in range(len(coords[0])):
            values = [c[axis] for c in coords]
            size = len(set(values))
            if size > 1:
                stride = next(i for i in range(count) if values[i] != values[0])
                found.append((stride, size))
        sizes = [size for _, size in sorted(found, reverse=True)]
    if math.prod(sizes) != count or len(sizes) > 3:
        sizes = [count // 4, 2, 2] if count % 4 == 0 else [count]
    return tuple([1] * (3 - len(sizes)) + sizes)


def kernel(dims, layers, batches, share, depth, width, latents, names, *refs):
    ref = dict(zip(names, refs))
    count = math.prod(dims)
    part = width // PARTS
    tile = part // 3 if part % 384 == 0 else part
    tiles = part // tile
    rows = count * share
    per_layer = count // layers
    layer, place = lax.axis_index("layer"), lax.axis_index("dict")
    mine = (place // (dims[1] * dims[2]), place // dims[2] % dims[1], place % dims[2])
    strides = (dims[1] * dims[2], dims[2], 1)
    orders = ((2, 1, 0), (1, 2, 0))

    def peer_of(axis, step):
        other = lax.rem(mine[axis] + step, dims[axis])
        return other, (layer, place + (other - mine[axis]) * strides[axis])

    def layer_peer(step):
        other = lax.rem(layer + step, layers)
        return other, (other, place)

    used = [0]

    def send(src, dst, device):
        slot = used[0]
        used[0] += 1
        copy = pltpu.make_async_remote_copy(
            src_ref=src,
            dst_ref=dst,
            send_sem=ref["send"].at[slot],
            recv_sem=ref["recv"].at[slot],
            device_id=device,
            device_id_type=pl.DeviceIdType.MESH,
        )
        copy.start()
        return copy

    loads = {}
    for slot, name in enumerate(("hidden", "w_down", "w_enc", "w_dec")):
        loads[name] = pltpu.make_async_copy(ref[name].at[0], ref[name + "_v"], ref["load"].at[slot])
        loads[name].start()

    barrier = pltpu.get_barrier_semaphore()
    peers = [peer_of(axis, step)[1] for axis in range(3) for step in range(1, dims[axis])]
    peers += [layer_peer(step)[1] for step in range(1, layers)]
    for device in peers:
        pl.semaphore_signal(barrier, inc=1, device_id=device, device_id_type=pl.DeviceIdType.MESH)

    at = lax.broadcasted_iota(I32, (count * batches * share,) * 2, 0)
    picked = jnp.where(at == ref["row_list"][...], 1.0, 0.0).T.astype(BF16)
    loads["hidden"].wait()
    chosen = jnp.dot(picked, ref["hidden_v"][...], preferred_element_type=F32).astype(BF16)
    ref["chosen"][...] = chosen.reshape(count, batches, share, depth)
    loads["w_down"].wait()
    pl.semaphore_wait(barrier, len(peers))

    def whole(axes):
        return tuple(pl.ds(mine[a], 1) if a in axes else slice(None) for a in range(3))

    def spread(b, c, phase, product):
        wide, narrow = ref[f"wide{b}{c}"], ref[f"narrow{b}{c}{phase}"]

        def step(j, carry):
            at = pl.multiple_of(j * tile, 128)
            value = product(pl.multiple_of(c * part + at, 128)).reshape(dims + (share, tile))
            wide[:, :, :, :, pl.ds(at, tile)] = value
            narrow[:, :, :, :, pl.ds(at, tile)] = value.astype(BF16)
            return carry

        lax.fori_loop(0, tiles, step, 0)
        return send_stage(b, c, phase, 0, narrow)

    def send_stage(b, c, phase, stage, source):
        axis = orders[c][stage]
        copies = []
        for step in range(1, dims[axis]):
            other, device = peer_of(axis, step)
            index = tuple(pl.ds(other, 1) if a == axis else slice(None) for a in range(3))
            copies.append(send(source.at[index], ref[f"in{b}{c}{phase}{stage}"].at[step - 1], device))
        return copies

    def add_stage(b, c, phase, stage, copies):
        axis = orders[c][stage]
        own = ref[f"wide{b}{c}"] if stage == 0 else ref[f"sum{b}{c}{stage - 1}"]
        index = tuple(pl.ds(mine[a], 1) if a == axis else slice(None) for a in range(3))
        for copy in copies:
            copy.wait_recv()
        total = own[index]
        for step in range(dims[axis] - 1):
            total = total + ref[f"in{b}{c}{phase}{stage}"][step].astype(F32)
        return total

    def reduce_rows(b, phase, copies, sent):
        for stage in range(2):
            yield
            following = []
            for c in range(PARTS):
                total = add_stage(b, c, phase, stage, copies[c])
                ref[f"sum{b}{c}{stage}"][...] = total
                out = ref[f"out{b}{c}{phase}{stage}"]
                out[...] = total.astype(BF16)
                following.append(send_stage(b, c, phase, stage + 1, out))
            sent += copies[0] + copies[1]
            copies = following
        yield
        sent += copies[0] + copies[1]
        return [add_stage(b, c, phase, 2, copies[c]) for c in range(PARTS)]

    def gather_stage(b, c, phase, stage):
        axes = [orders[c][s] for s in range(stage + 1)]
        block = ref[f"all{b}{c}{phase}"].at[whole(axes)]
        axis = orders[c][stage]
        return [send(block, block, peer_of(axis, step)[1]) for step in range(1, dims[axis])]

    def gather_rows(b, phase, copies, sent):
        for stage in (1, 0):
            yield
            following = []
            for c in range(PARTS):
                for copy in copies[c]:
                    copy.wait_recv()
                following.append(gather_stage(b, c, phase, stage))
            sent += copies[0] + copies[1]
            copies = following
        yield
        for c in range(PARTS):
            for copy in copies[c]:
                copy.wait_recv()
        sent += copies[0] + copies[1]

    alive = ref["alive"][...].astype(F32)

    def chain(b, sent):
        lhs = ref["chosen"][:, b].reshape(rows, depth)
        copies = [
            spread(b, c, 0, lambda at: jnp.dot(lhs, ref["w_down_v"][:, pl.ds(at, tile)], preferred_element_type=F32))
            for c in range(PARTS)
        ]
        if b == batches - 1:
            loads["w_dec"].wait()

            def split(i, carry):
                at = pl.ds(pl.multiple_of(i * 64, 64), 64)
                value = ref["w_dec_v"][at, :]
                high = value.astype(BF16)
                ref["high"][at, :] = high
                ref["low"][at, :] = (value - high.astype(F32)).astype(BF16)
                return carry

            lax.fori_loop(0, latents // 64, split, 0)
            loads["w_enc"].wait()
        totals = yield from reduce_rows(b, 0, copies, sent)
        copies = []
        for c in range(PARTS):
            ref[f"all{b}{c}0"][whole((0, 1, 2))] = totals[c].astype(BF16)
            copies.append(gather_stage(b, c, 0, 2))
        yield from gather_rows(b, 0, copies, sent)
        encoded = ref[f"encoded{b}"]
        for c in range(PARTS):
            acts = ref[f"all{b}{c}0"][...].reshape(rows, part)
            term = jnp.dot(acts, ref["w_enc_v"][c * part:(c + 1) * part, :], preferred_element_type=F32)
            encoded[...] = term if c == 0 else encoded[...] + term
        copies = [send(encoded, ref[f"encoded_in{b}"].at[s - 1], layer_peer(s)[1]) for s in range(1, layers)]
        yield
        for copy in copies:
            copy.wait_recv()
        sent += copies
        preact = encoded[...]
        for s in range(layers - 1):
            preact = preact + ref[f"encoded_in{b}"][s]
        preact = preact + ref["b_enc"][...]
        latent = (jnp.maximum(preact, 0.0) * alive).astype(BF16)
        ref[f"latent{b}"][...] = latent.reshape(count, share, latents)
        ref["latent_out"][:, b] = ref[f"latent{b}"][pl.ds(layer * per_layer, per_layer)]

        def decode(at):
            left = ref[f"latent{b}"][...].reshape(rows, latents)
            return jnp.dot(left, ref["high"][:, pl.ds(at, tile)], preferred_element_type=F32) + jnp.dot(
                left, ref["low"][:, pl.ds(at, tile)], preferred_element_type=F32
            )

        copies = [spread(b, c, 1, decode) for c in range(PARTS)]
        totals = yield from reduce_rows(b, 1, copies, sent)
        copies = []
        for c in range(PARTS):
            own = ref[f"all{b}{c}0"][whole((0, 1, 2))].reshape(share, part).astype(F32)
            columns = slice(c * part, (c + 1) * part)
            residual = own - (totals[c].reshape(share, part) + ref["b_dec"][:, columns])
            ref["residual_out"][b, :, columns] = residual
            ref[f"all{b}{c}1"][whole((0, 1, 2))] = residual.astype(BF16).reshape(1, 1, 1, share, part)
            copies.append(gather_stage(b, c, 1, 2))
        yield from gather_rows(b, 1, copies, sent)
        back = ref[f"back{b}"]
        for c in range(PARTS):
            left = ref[f"all{b}{c}1"][...].reshape(rows, part)
            columns = slice(c * part, (c + 1) * part)
            contract = (((1,), (1,)), ((), ()))
            term = lax.dot_general(left, ref["high"][:, columns], contract, preferred_element_type=F32)
            term = term + lax.dot_general(left, ref["low"][:, columns], contract, preferred_element_type=F32)
            term = term.reshape(count, share, latents)
            back[...] = term if c == 0 else back[...] + term
        copies = []
        for s in range(1, layers):
            other, device = layer_peer(s)
            block = back.at[pl.ds(other * per_layer, per_layer)]
            copies.append(send(block, ref[f"back_in{b}"].at[s - 1], device))
        yield
        for copy in copies:
            copy.wait_recv()
        sent += copies
        total = back[pl.ds(layer * per_layer, per_layer)]
        for s in range(layers - 1):
            total = total + ref[f"back_in{b}"][s]
        ref["adjoint_out"][:, b] = -total * alive[None]

    sent = []
    running = [chain(b, sent) for b in range(batches)]
    while running:
        for item in list(running):
            if next(item, running) is running:
                running.remove(item)
    for copy in sent:
        copy.wait_send()


def per_device(dims, layers, hidden, row_list, w_down, w_enc, b_enc, w_dec, b_dec, alive_mask):
    count = math.prod(dims)
    _, row_count, depth = hidden.shape
    width, latents = w_enc.shape[1:]
    part = width // PARTS
    batches = 2 if row_count // count % 32 == 0 else 1
    share = row_count // count // batches
    rows = count * share
    orders = ((2, 1, 0), (1, 2, 0))

    scratch = {
        "hidden_v": pltpu.VMEM((row_count, depth), BF16),
        "w_down_v": pltpu.VMEM((depth, width), BF16),
        "w_enc_v": pltpu.VMEM((width, latents), BF16),
        "w_dec_v": pltpu.VMEM((latents, width), F32),
        "high": pltpu.VMEM((latents, width), BF16),
        "low": pltpu.VMEM((latents, width), BF16),
        "chosen": pltpu.VMEM((count, batches, share, depth), BF16),
    }
    for b in range(batches):
        scratch[f"encoded{b}"] = pltpu.VMEM((rows, latents), F32)
        scratch[f"encoded_in{b}"] = pltpu.VMEM((max(layers - 1, 1), rows, latents), F32)
        scratch[f"latent{b}"] = pltpu.VMEM((count, share, latents), BF16)
        scratch[f"back{b}"] = pltpu.VMEM((count, share, latents), F32)
        scratch[f"back_in{b}"] = pltpu.VMEM((max(layers - 1, 1), count // layers, share, latents), F32)
        for c in range(PARTS):
            scratch[f"wide{b}{c}"] = pltpu.VMEM(dims + (share, part), F32)
            for phase in range(2):
                scratch[f"narrow{b}{c}{phase}"] = pltpu.VMEM(dims + (share, part), BF16)
                scratch[f"all{b}{c}{phase}"] = pltpu.VMEM(dims + (share, part), BF16)
            left = list(dims)
            for stage, axis in enumerate(orders[c]):
                steps = max(left[axis] - 1, 1)
                left[axis] = 1
                for phase in range(2):
                    scratch[f"in{b}{c}{phase}{stage}"] = pltpu.VMEM((steps, *left, share, part), BF16)
                    if stage < 2:
                        scratch[f"out{b}{c}{phase}{stage}"] = pltpu.VMEM((*left, share, part), BF16)
                if stage < 2:
                    scratch[f"sum{b}{c}{stage}"] = pltpu.VMEM((*left, share, part), F32)
    copies = 4 * batches * PARTS * sum(d - 1 for d in dims) + 2 * batches * (layers - 1)
    scratch["load"] = pltpu.SemaphoreType.DMA((4,))
    scratch["send"] = pltpu.SemaphoreType.DMA((copies,))
    scratch["recv"] = pltpu.SemaphoreType.DMA((copies,))

    names = ("hidden", "w_down", "w_enc", "w_dec", "row_list", "b_enc", "b_dec", "alive")
    names += ("latent_out", "residual_out", "adjoint_out") + tuple(scratch)
    vmem = pl.BlockSpec(memory_space=pltpu.VMEM)
    hbm = pl.BlockSpec(memory_space=pl.ANY)
    own = (count // layers, batches, share, latents)
    latent, residual, adjoint = pl.pallas_call(
        functools.partial(kernel, dims, layers, batches, share, depth, width, latents, names),
        out_shape=(
            jax.ShapeDtypeStruct(own, BF16),
            jax.ShapeDtypeStruct((batches, share, width), F32),
            jax.ShapeDtypeStruct(own, F32),
        ),
        in_specs=[hbm] * 4 + [vmem] * 4,
        out_specs=(vmem, vmem, vmem),
        scratch_shapes=list(scratch.values()),
        compiler_params=pltpu.CompilerParams(
            collective_id=0, has_side_effects=True, vmem_limit_bytes=62 * 1024 * 1024
        ),
    )(hidden, w_down, w_enc, w_dec, row_list[None], b_enc[None], b_dec, alive_mask[None])
    return (
        latent.reshape(-1, latents),
        residual.reshape(1, -1, width),
        adjoint.reshape(-1, latents),
    )


def solution(mesh):
    return jax.shard_map(
        functools.partial(per_device, digits_of(mesh), mesh.shape["layer"]),
        mesh=mesh,
        in_specs=(
            P("layer", None, "dict"),
            P(),
            P("layer", "dict", None),
            P("layer", None, "dict"),
            P("dict"),
            P("layer", "dict", None),
            P("layer", None),
            P("dict"),
        ),
        out_specs=(P("layer", "dict"), P("layer", "dict", None), P("layer", "dict")),
        check_vma=False,
    )
```

time: 474 us -> 141 us (0.30)
  the two profiles are of different devices: /device:TPU:1 before, /device:TPU:31 now
where the time goes in v1:
time: 141 us; the launch traced here: 140 us
  Pallas kernels  132 us (94%)
  local copies, waits for them, and re-layouts  7.38 us (5%)
    pallas_call x1, Pallas kernels, per_device(): pl.pallas_call(functools.partial(kernel, dims, layers, batches, share, de...  132 us
    unnamed x4, local copies, waits for them, and re-layouts  7.38 us

profile of v1, /device:TPU:31, one launch (start us, length us, event | category | flops | bytes accessed | tf_op | source)
XLA Modules:
  0.0 140.4 jit_solution(15297385329134356717)
XLA Ops:
  0.6 2.2 %copy.11.refs_0_ = bf16[1,512,576]{2,1,0:T(8,128)(2,1)} copy(bf16[1,512,576]{1,2,0:T(8,128)(2,1)} %param.8) | data formatting | bytes 1179648 | tf_op args[0]
  2.8 132.4 %shard_map.103 = (bf16[8,2,16,512]{3,2,1,0:T(8,128)(2,1)}, f32[2,16,2304]{2,1,0:T(8,128)}, f32[8,2,16,512]{3,2,1,0:T(8,128)}) custom-call(bf16[1,512,576]{2,1,0:T(8,128)(2,1)} %copy.11.refs_0_, bf16[1,576,2304]{2,1,0:T(8,128)(2,1)} %refs_1_.1, bf16[1,2304,512]{2,1,0:T(8,128)(2,1)} %refs_2_.1, f32[1,512,2304]{2,1,0:T(8,128)} %refs_3_.1, s32[1,512]{1,0:T(1,128)} %bitcast.9, ...), custom_call_target="tpu_custom_call" | custom-call | tf_op jit(solution)/shard_map/pallas_call | solution.py:312
  135.2 1.7 %copy.15 = bf16[256,512]{1,0:T(8,128)(2,1)} copy(bf16[256,512]{1,0:T(8,128)(2,1)} %bitcast.8) | data formatting | bytes 524288
  136.9 1.7 %copy.16 = f32[1,32,2304]{2,1,0:T(8,128)} copy(f32[1,32,2304]{2,1,0:T(8,128)} %bitcast.7) | data formatting | bytes 589824
  138.6 1.9 %copy.17 = f32[256,512]{1,0:T(8,128)} copy(f32[256,512]{1,0:T(8,128)} %bitcast.6) | data formatting | bytes 1048576

commit v2 on v1

v2 whole, which is shorter than its diff:
```python
import functools
import itertools
import math

import jax
import jax.numpy as jnp
from jax import lax
from jax.experimental import pallas as pl
from jax.experimental.pallas import tpu as pltpu
from jax.sharding import PartitionSpec as P

F32, BF16, I32 = jnp.float32, jnp.bfloat16, jnp.int32
ORDERS = ((2, 1, 0), (1, 2, 0))
RATE, HOP, LOCAL, MATH = 1e5, 1.5, 6e5, 6e8


def digits_of(mesh):
    line = list(mesh.devices.reshape(mesh.shape["layer"], -1)[0])
    count = len(line)
    try:
        coords = [tuple(d.coords) for d in line]
    except (AttributeError, TypeError):
        coords = None
    sizes = []
    if coords:
        found = []
        for axis in range(len(coords[0])):
            values = [c[axis] for c in coords]
            size = len(set(values))
            if size > 1:
                stride = next(i for i in range(count) if values[i] != values[0])
                found.append((stride, size))
        sizes = [size for _, size in sorted(found, reverse=True)]
    if math.prod(sizes) != count or len(sizes) > 3:
        sizes = [count // 4, 2, 2] if count % 4 == 0 else [count]
    return tuple([1] * (3 - len(sizes)) + sizes)


def kernel(dims, layers, batches, pairs, share, depth, width, latents, names, *refs):
    ref = dict(zip(names, refs))
    count = math.prod(dims)
    part = width // (2 * pairs)
    rows = count * share
    per_layer = count // layers
    layer, place = lax.axis_index("layer"), lax.axis_index("dict")
    mine = (place // (dims[1] * dims[2]), place // dims[2] % dims[1], place % dims[2])
    strides = (dims[1] * dims[2], dims[2], 1)
    free, clock, used = {axis: 0.0 for axis in (0, 1, 2, "layer")}, [0.0], [0]
    sent, active, waiting, ended = [], [], [], {}

    def spend(operations):
        clock[0] += 0.1 + operations / MATH

    def busy(link, length, rate):
        free[link] = max(free[link], clock[0]) + length / rate
        return free[link] + HOP

    def peer_of(axis, step):
        other = lax.rem(mine[axis] + step, dims[axis])
        return other, (layer, place + (other - mine[axis]) * strides[axis])

    def layer_peer(step):
        other = lax.rem(layer + step, layers)
        return other, (other, place)

    def send(src, dst, device):
        slot = used[0]
        used[0] += 1
        copy = pltpu.make_async_remote_copy(
            src_ref=src,
            dst_ref=dst,
            send_sem=ref["send"].at[slot],
            recv_sem=ref["recv"].at[slot],
            device_id=device,
            device_id_type=pl.DeviceIdType.MESH,
        )
        copy.start()
        sent.append(copy)
        return copy

    loads = {}
    for slot, name in enumerate(("hidden", "w_down", "w_enc", "w_dec")):
        loads[name] = pltpu.make_async_copy(ref[name].at[0], ref[name + "_v"], ref["load"].at[slot])
        loads[name].start()

    barrier = pltpu.get_barrier_semaphore()
    peers = [peer_of(axis, step)[1] for axis in range(3) for step in range(1, dims[axis])]
    peers += [layer_peer(step)[1] for step in range(1, layers)]
    for device in peers:
        pl.semaphore_signal(barrier, inc=1, device_id=device, device_id_type=pl.DeviceIdType.MESH)

    at = lax.broadcasted_iota(I32, (count * batches * share,) * 2, 0)
    picked = jnp.where(at == ref["row_list"][...], 1.0, 0.0).T.astype(BF16)
    loads["hidden"].wait()
    last = (((1,), (1,)), ((), ()))
    chosen = lax.dot_general(picked, ref["hidden_v"][...], last, preferred_element_type=F32).astype(BF16)
    ref["chosen"][...] = chosen.reshape(count, batches, share, depth)
    loads["w_down"].wait()
    pl.semaphore_wait(barrier, len(peers))

    def block_of(axes):
        return tuple(pl.ds(mine[a], 1) if a in axes else slice(None) for a in range(3))

    def stage_cost(axis, blocks):
        across = (dims[axis] // 2) * ((dims[axis] + 1) // 2)
        return busy(axis, across * 2 * blocks * share * part * 2, RATE)

    def send_stage(key, side, stage, source):
        axis = ORDERS[side][stage]
        copies = []
        for step in range(1, dims[axis]):
            other, device = peer_of(axis, step)
            index = tuple(pl.ds(other, 1) if a == axis else slice(None) for a in range(3))
            copies.append(send(source.at[index], ref[f"in{key}{stage}"].at[step - 1], device))
        left = math.prod(dims[a] for a in ORDERS[side][stage + 1 :])
        return copies, stage_cost(axis, left)

    def add_stage(key, side, stage, copies):
        axis = ORDERS[side][stage]
        own = ref[f"wide{key[:-1]}"] if stage == 0 else ref[f"sum{key[:-1]}{stage - 1}"]
        for copy in copies:
            copy.wait_recv()
        total = own[block_of((axis,))]
        for step in range(dims[axis] - 1):
            total = total + ref[f"in{key}{stage}"][step].astype(F32)
        return total

    def gather_stage(key, side, stage):
        block = ref[f"all{key}"].at[block_of(ORDERS[side][: stage + 1])]
        axis = ORDERS[side][stage]
        copies = [send(block, block, peer_of(axis, step)[1]) for step in range(1, dims[axis])]
        left = math.prod(dims[a] for a in ORDERS[side][stage + 1 :])
        return copies, stage_cost(axis, left)

    def columns_of(pair):
        return slice(pair * 2 * part, (pair + 1) * 2 * part)

    def exchange(b, pair, phase, value, own_block):
        keys = [f"{b}_{pair}{side}{phase}" for side in range(2)]
        state = []
        for side, key in enumerate(keys):
            term = value[:, side * part : (side + 1) * part].reshape(dims + (share, part))
            ref[f"wide{key[:-1]}"][...] = term
            ref[f"narrow{key}"][...] = term.astype(BF16)
            state.append(send_stage(key, side, 0, ref[f"narrow{key}"]))
        for stage in range(2):
            yield max(ready for _, ready in state)
            following = []
            for side, key in enumerate(keys):
                total = add_stage(key, side, stage, state[side][0])
                ref[f"sum{key[:-1]}{stage}"][...] = total
                ref[f"out{key}{stage}"][...] = total.astype(BF16)
                following.append(send_stage(key, side, stage + 1, ref[f"out{key}{stage}"]))
            spend(0)
            state = following
        yield max(ready for _, ready in state)
        following = []
        for side, key in enumerate(keys):
            total = add_stage(key, side, 2, state[side][0]).reshape(share, part)
            start = (2 * pair + side) * part
            block = own_block(f"{b}_{pair}{side}", total, slice(start, start + part))
            ref[f"all{key}"][block_of((0, 1, 2))] = block.reshape(1, 1, 1, share, part)
            following.append(gather_stage(key, side, 2))
        spend(0)
        state = following
        for stage in (1, 0):
            yield max(ready for _, ready in state)
            following = []
            for side, key in enumerate(keys):
                for copy in state[side][0]:
                    copy.wait_recv()
                following.append(gather_stage(key, side, stage))
            state = following
        yield max(ready for _, ready in state)
        for copies, _ in state:
            for copy in copies:
                copy.wait_recv()

    def gathered(b, pair, phase):
        sides = [ref[f"all{b}_{pair}{side}{phase}"][...].reshape(rows, part) for side in range(2)]
        return jnp.concatenate(sides, axis=1)

    def split():
        loads["w_dec"].wait()

        def step(i, carry):
            at = pl.ds(pl.multiple_of(i * 64, 64), 64)
            value = ref["w_dec_v"][at, :]
            high = value.astype(BF16)
            ref["high"][at, :] = high
            ref["low"][at, :] = (value - high.astype(F32)).astype(BF16)
            return carry

        lax.fori_loop(0, latents // 64, step, 0)
        loads["w_enc"].wait()
        spend(1e9)

    alive = ref["alive"][...].astype(F32)

    def count_up(key):
        ended[key] = ended.get(key, 0) + 1
        return ended[key]

    def forward(b, pair):
        lhs = ref["chosen"][:, b].reshape(rows, depth)
        value = jnp.dot(lhs, ref["w_down_v"][:, columns_of(pair)], preferred_element_type=F32)
        spend(2 * rows * depth * 2 * part)
        yield from exchange(b, pair, 0, value, lambda key, total, columns: total.astype(BF16))
        if not ended:
            split()
        term = jnp.dot(gathered(b, pair, 0), ref["w_enc_v"][columns_of(pair), :], preferred_element_type=F32)
        spend(2 * rows * latents * 2 * part)
        encoded = ref[f"encoded{b}"]
        number = count_up((b, 0))
        encoded[...] = term if number == 1 else encoded[...] + term
        if number < pairs:
            return
        copies = [send(encoded, ref[f"encoded_in{b}"].at[s - 1], layer_peer(s)[1]) for s in range(1, layers)]
        yield busy("layer", rows * latents * 4 * (layers - 1), LOCAL)
        for copy in copies:
            copy.wait_recv()
        preact = encoded[...]
        for s in range(layers - 1):
            preact = preact + ref[f"encoded_in{b}"][s]
        preact = preact + ref["b_enc"][...]
        latent = (jnp.maximum(preact, 0.0) * alive).astype(BF16)
        ref[f"latent{b}"][...] = latent.reshape(count, share, latents)
        ref["latent_out"][:, b] = ref[f"latent{b}"][pl.ds(layer * per_layer, per_layer)]
        spend(0)
        waiting.extend(backward(b, later) for later in range(pairs))

    def backward(b, pair):
        left = ref[f"latent{b}"][...].reshape(rows, latents)
        columns = columns_of(pair)
        value = jnp.dot(left, ref["high"][:, columns], preferred_element_type=F32)
        value = value + jnp.dot(left, ref["low"][:, columns], preferred_element_type=F32)
        spend(4 * rows * latents * 2 * part)

        def residual_block(key, total, columns):
            own = ref[f"all{key}0"][block_of((0, 1, 2))].reshape(share, part).astype(F32)
            residual = own - (total + ref["b_dec"][:, columns])
            ref["residual_out"][b, :, columns] = residual
            return residual.astype(BF16)

        yield from exchange(b, pair, 1, value, residual_block)
        wide = gathered(b, pair, 1)
        term = lax.dot_general(wide, ref["high"][:, columns], last, preferred_element_type=F32)
        term = term + lax.dot_general(wide, ref["low"][:, columns], last, preferred_element_type=F32)
        term = term.reshape(count, share, latents)
        spend(4 * rows * latents * 2 * part)
        back = ref[f"back{b}"]
        number = count_up((b, 1))
        back[...] = term if number == 1 else back[...] + term
        if number < pairs:
            return
        copies = []
        for s in range(1, layers):
            other, device = layer_peer(s)
            block = back.at[pl.ds(other * per_layer, per_layer)]
            copies.append(send(block, ref[f"back_in{b}"].at[s - 1], device))
        yield busy("layer", rows * latents * 4 * (layers - 1) // layers, LOCAL)
        for copy in copies:
            copy.wait_recv()
        total = back[pl.ds(layer * per_layer, per_layer)]
        for s in range(layers - 1):
            total = total + ref[f"back_in{b}"][s]
        ref["adjoint_out"][:, b] = -total * alive[None]
        spend(0)

    waiting.extend(forward(b, pair) for b in range(batches) for pair in range(pairs))
    while active or waiting:
        active.sort(key=lambda entry: entry[0])
        if waiting and (not active or max(free[1], free[2]) <= max(active[0][0], clock[0])):
            item = waiting.pop(0)
        else:
            ready, _, item = active.pop(0)
            clock[0] = max(clock[0], ready)
        ready = next(item, None)
        if ready is not None:
            active.append((ready, len(active), item))
    for copy in sent:
        copy.wait_send()


def copy_kernel(first, second, third, first_out, second_out, third_out, sem):
    copies = [
        pltpu.make_async_copy(source, target, sem.at[slot])
        for slot, (source, target) in enumerate(((first, first_out), (second, second_out), (third, third_out)))
    ]
    for copy in copies:
        copy.start()
    for copy in copies:
        copy.wait()


def per_device(dims, layers, hidden, row_list, w_down, w_enc, b_enc, w_dec, b_dec, alive_mask):
    count = math.prod(dims)
    hidden = jnp.swapaxes(hidden, 1, 2)
    _, depth, row_count = hidden.shape
    width, latents = w_enc.shape[1:]
    pairs = 3 if width % 768 == 0 else 1
    part = width // (2 * pairs)
    batches = 2 if row_count // count % 32 == 0 else 1
    share = row_count // count // batches
    rows = count * share

    scratch = {
        "hidden_v": pltpu.VMEM((depth, row_count), BF16),
        "w_down_v": pltpu.VMEM((depth, width), BF16),
        "w_enc_v": pltpu.VMEM((width, latents), BF16),
        "w_dec_v": pltpu.VMEM((latents, width), F32),
        "high": pltpu.VMEM((latents, width), BF16),
        "low": pltpu.VMEM((latents, width), BF16),
        "chosen": pltpu.VMEM((count, batches, share, depth), BF16),
    }
    for b in range(batches):
        scratch[f"encoded{b}"] = pltpu.VMEM((rows, latents), F32)
        scratch[f"encoded_in{b}"] = pltpu.VMEM((max(layers - 1, 1), rows, latents), F32)
        scratch[f"latent{b}"] = pltpu.VMEM((count, share, latents), BF16)
        scratch[f"back{b}"] = pltpu.VMEM((count, share, latents), F32)
        scratch[f"back_in{b}"] = pltpu.VMEM((max(layers - 1, 1), count // layers, share, latents), F32)
        for pair, side in itertools.product(range(pairs), range(2)):
            key = f"{b}_{pair}{side}"
            scratch[f"wide{key}"] = pltpu.VMEM(dims + (share, part), F32)
            for phase in range(2):
                scratch[f"narrow{key}{phase}"] = pltpu.VMEM(dims + (share, part), BF16)
                scratch[f"all{key}{phase}"] = pltpu.VMEM(dims + (share, part), BF16)
            left = list(dims)
            for stage, axis in enumerate(ORDERS[side]):
                left[axis] = 1
                for phase in range(2):
                    shape = (max(dims[axis] - 1, 1), *left, share, part)
                    scratch[f"in{key}{phase}{stage}"] = pltpu.VMEM(shape, BF16)
                    if stage < 2:
                        scratch[f"out{key}{phase}{stage}"] = pltpu.VMEM((*left, share, part), BF16)
                if stage < 2:
                    scratch[f"sum{key}{stage}"] = pltpu.VMEM((*left, share, part), F32)
    copies = 8 * batches * pairs * sum(d - 1 for d in dims) + 2 * batches * (layers - 1)
    scratch["load"] = pltpu.SemaphoreType.DMA((4,))
    scratch["send"] = pltpu.SemaphoreType.DMA((copies,))
    scratch["recv"] = pltpu.SemaphoreType.DMA((copies,))

    names = ("hidden", "w_down", "w_enc", "w_dec", "row_list", "b_enc", "b_dec", "alive")
    names += ("latent_out", "residual_out", "adjoint_out") + tuple(scratch)
    vmem = pl.BlockSpec(memory_space=pltpu.VMEM)
    hbm = pl.BlockSpec(memory_space=pl.ANY)
    own = (count // layers, batches, share, latents)
    latent, residual, adjoint = pl.pallas_call(
        functools.partial(kernel, dims, layers, batches, pairs, share, depth, width, latents, names),
        out_shape=(
            jax.ShapeDtypeStruct(own, BF16),
            jax.ShapeDtypeStruct((batches, share, width), F32),
            jax.ShapeDtypeStruct(own, F32),
        ),
        in_specs=[hbm] * 4 + [vmem] * 4,
        out_specs=(vmem, vmem, vmem),
        scratch_shapes=list(scratch.values()),
        compiler_params=pltpu.CompilerParams(
            collective_id=0, has_side_effects=True, vmem_limit_bytes=62 * 1024 * 1024
        ),
    )(hidden, w_down, w_enc, w_dec, row_list[None], b_enc[None], b_dec, alive_mask[None])
    results = (latent.reshape(-1, latents), residual.reshape(1, -1, width), adjoint.reshape(-1, latents))
    return tuple(
        pl.pallas_call(
            copy_kernel,
            out_shape=tuple(jax.ShapeDtypeStruct(a.shape, a.dtype) for a in results),
            in_specs=[hbm] * 3,
            out_specs=(hbm,) * 3,
            scratch_shapes=[pltpu.SemaphoreType.DMA((3,))],
        )(*results)
    )


def solution(mesh):
    return jax.shard_map(
        functools.partial(per_device, digits_of(mesh), mesh.shape["layer"]),
        mesh=mesh,
        in_specs=(
            P("layer", None, "dict"),
            P(),
            P("layer", "dict", None),
            P("layer", None, "dict"),
            P("dict"),
            P("layer", "dict", None),
            P("layer", None),
            P("dict"),
        ),
        out_specs=(P("layer", "dict"), P("layer", "dict", None), P("layer", "dict")),
        check_vma=False,
    )
```

time: 141 us -> 141 us (level)
  the two profiles are of different devices: /device:TPU:31 before, /device:TPU:1 now
where the time goes in v2:
time: 141 us; the launch traced here: 140 us
  Pallas kernels  140 us (99%)
    pallas_call x1, Pallas kernels, per_device(): pl.pallas_call(functools.partial(kernel, dims, layers, batches, pairs, sh...  106 us
    pallas_call x1, Pallas kernels, per_device(): pl.pallas_call(copy_kernel, out_shape=tuple((jax.ShapeDtypeStruct(a.shape...  33.9 us

profile of v2, /device:TPU:1, one launch (start us, length us, event | category | flops | bytes accessed | tf_op | source)
XLA Modules:
  0.0 140.3 jit_solution(2011100447600332708)
XLA Ops:
  0.6 105.6 %shard_map.103 = (bf16[8,2,16,512]{3,2,1,0:T(8,128)(2,1)}, f32[2,16,2304]{2,1,0:T(8,128)}, f32[8,2,16,512]{3,2,1,0:T(8,128)}) custom-call(bf16[1,576,512]{2,1,0:T(8,128)(2,1)} %bitcast.7, bf16[1,576,2304]{2,1,0:T(8,128)(2,1)} %refs_1_.1, bf16[1,2304,512]{2,1,0:T(8,128)(2,1)} %refs_2_.1, f32[1,512,2304]{2,1,0:T(8,128)} %refs_3_.1, s32[1,512]{1,0:T(1,128)} %bitcast.11, ...), custom_call_target="tpu_custom_call" | custom-call | tf_op jit(solution)/shard_map/pallas_call | solution.py:348
  106.3 33.9 %shard_map.104 = (bf16[256,512]{1,0:T(8,128)(2,1)}, f32[1,32,2304]{2,1,0:T(8,128)}, f32[256,512]{1,0:T(8,128)}) custom-call(bf16[256,512]{1,0:T(8,128)(2,1)} %bitcast.10, f32[1,32,2304]{2,1,0:T(8,128)} %bitcast.9, f32[256,512]{1,0:T(8,128)} %bitcast.8), custom_call_target="tpu_custom_call" | custom-call | tf_op jit(solution)/shard_map/pallas_call | solution.py:364

commit v3 on v2

v3 whole, which is shorter than its diff:
```python
import functools
import math

import jax
import jax.numpy as jnp
from jax import lax
from jax.experimental import pallas as pl
from jax.experimental.pallas import tpu as pltpu
from jax.sharding import PartitionSpec as P

F32, BF16, I32 = jnp.float32, jnp.bfloat16, jnp.int32
RATE, HOP, LOCAL, MATH = 9e4, 2.0, 6e5, 4e8
SLACK = 1.0


def digits_of(mesh):
    line = list(mesh.devices.reshape(mesh.shape["layer"], -1)[0])
    count = len(line)
    try:
        coords = [tuple(d.coords) for d in line]
    except (AttributeError, TypeError):
        coords = None
    sizes = []
    if coords:
        found = []
        for axis in range(len(coords[0])):
            values = [c[axis] for c in coords]
            size = len(set(values))
            if size > 1:
                stride = next(i for i in range(count) if values[i] != values[0])
                found.append((stride, size))
        sizes = [size for _, size in sorted(found, reverse=True)]
    if math.prod(sizes) != count or len(sizes) > 3:
        sizes = [count // 4, 2, 2] if count % 4 == 0 else [count]
    sizes = [1] * (3 - len(sizes)) + sizes
    if sizes[0] == 4 and sizes[1:] == [2, 2]:
        sizes = [2, 2, 2, 2]
    return tuple(sizes)


def orders_of(dims):
    if len(dims) == 4:
        return ((3, 2, 1, 0), (2, 3, 1, 0), (1, 0, 3, 2))
    return ((2, 1, 0), (1, 2, 0), (0, 2, 1))


def cuts_of(width):
    if width % 768 or width < 2304:
        return (((0, 0, width),),)
    groups, start = [], 0
    for group in range(width // 768):
        kinds = ((2, 256), (0, 256), (1, 256)) if group % 3 < 2 else ((0, 384), (1, 384))
        parts = []
        for kind, columns in kinds:
            parts.append((kind, start, columns))
            start += columns
        groups.append(tuple(parts))
    return tuple(groups)


def kernel(dims, cuts, layers, batches, share, depth, width, latents, names, *refs):
    ref = dict(zip(names, refs))
    count = math.prod(dims)
    orders, axes = orders_of(dims), range(len(dims))
    pairs = len(cuts)
    rows = count * share
    per_layer = count // layers
    layer, place = lax.axis_index("layer"), lax.axis_index("dict")
    strides = tuple(math.prod(dims[axis + 1 :]) for axis in axes)
    mine = tuple(place // strides[axis] % dims[axis] for axis in axes)
    free, clock, used = {link: 0.0 for link in (*axes, "middle", "layer")}, [0.0], [0]
    sent, active, waiting, ended = [], [], [], {}

    def spend(operations):
        clock[0] += 0.1 + operations / MATH

    def busy(link, length, rate):
        free[link] = max(free[link], clock[0]) + length / rate
        return free[link] + HOP

    def peer_of(axis, step):
        other = lax.rem(mine[axis] + step, dims[axis])
        return other, (layer, place + (other - mine[axis]) * strides[axis])

    def layer_peer(step):
        other = lax.rem(layer + step, layers)
        return other, (other, place)

    def send(src, dst, device):
        slot = used[0]
        used[0] += 1
        copy = pltpu.make_async_remote_copy(
            src_ref=src,
            dst_ref=dst,
            send_sem=ref["send"].at[slot],
            recv_sem=ref["recv"].at[slot],
            device_id=device,
            device_id_type=pl.DeviceIdType.MESH,
        )
        copy.start()
        sent.append(copy)
        return copy

    loads = {}
    for slot, name in enumerate(("hidden", "w_down", "w_enc", "w_dec")):
        loads[name] = pltpu.make_async_copy(ref[name].at[0], ref[name + "_v"], ref["load"].at[slot])
    loads["hidden"].start()
    loads["w_down"].start()

    barrier = pltpu.get_barrier_semaphore()
    peers = [peer_of(axis, step)[1] for axis in axes for step in range(1, dims[axis])]
    peers += [layer_peer(step)[1] for step in range(1, layers)]
    for device in peers:
        pl.semaphore_signal(barrier, inc=1, device_id=device, device_id_type=pl.DeviceIdType.MESH)

    at = lax.broadcasted_iota(I32, (count * batches * share,) * 2, 0)
    picked = jnp.where(at == ref["row_list"][...], 1.0, 0.0).T.astype(BF16)
    ref["picked"][...] = picked.reshape(count, batches, share, count * batches * share)
    last = (((1,), (1,)), ((), ()))
    loads["hidden"].wait()
    loads["w_down"].wait()
    loads["w_enc"].start()
    loads["w_dec"].start()
    pl.semaphore_wait(barrier, len(peers))

    def block_of(among):
        return tuple(pl.ds(mine[a], 1) if a in among else slice(None) for a in axes)

    def stage_cost(axis, blocks, columns):
        length = 2 * blocks * share * columns * 2
        if len(dims) == 4 and axis < 2:
            ready = busy(1, length, RATE)
            return ready if axis else max(ready, busy("middle", 2 * length, RATE))
        return busy(axis, length * (dims[axis] // 2) * ((dims[axis] + 1) // 2), RATE)

    def send_stage(key, part, stage, source):
        kind, _, columns = part
        axis = orders[kind][stage]
        copies = []
        for step in range(1, dims[axis]):
            other, device = peer_of(axis, step)
            index = tuple(pl.ds(other, 1) if a == axis else slice(None) for a in axes)
            copies.append(send(source.at[index], ref[f"in{key}{stage}"].at[step - 1], device))
        left = math.prod(dims[a] for a in orders[kind][stage + 1 :])
        return copies, stage_cost(axis, left, columns)

    def add_stage(key, part, stage, copies):
        axis = orders[part[0]][stage]
        own = ref[f"wide{key[:-1]}"] if stage == 0 else ref[f"sum{key[:-1]}{stage - 1}"]
        for copy in copies:
            copy.wait_recv()
        total = own[block_of((axis,))]
        for step in range(dims[axis] - 1):
            total = total + ref[f"in{key}{stage}"][step].astype(F32)
        return total

    def gather_stage(key, part, stage):
        kind, _, columns = part
        block = ref[f"all{key}"].at[block_of(orders[kind][: stage + 1])]
        axis = orders[kind][stage]
        copies = [send(block, block, peer_of(axis, step)[1]) for step in range(1, dims[axis])]
        left = math.prod(dims[a] for a in orders[kind][stage + 1 :])
        return copies, stage_cost(axis, left, columns)

    def columns_of(pair):
        return slice(cuts[pair][0][1], cuts[pair][-1][1] + cuts[pair][-1][2])

    def exchange(b, pair, phase, value, own_block):
        parts = [(f"{b}_{pair}{side}{phase}", part) for side, part in enumerate(cuts[pair])]
        state, final = [], len(dims) - 1
        for key, part in parts:
            start = part[1] - cuts[pair][0][1]
            term = value[:, start : start + part[2]].reshape(dims + (share, part[2]))
            ref[f"wide{key[:-1]}"][...] = term
            ref[f"narrow{key}"][...] = term.astype(BF16)
            state.append(send_stage(key, part, 0, ref[f"narrow{key}"]))
        for stage in range(final):
            yield max(ready for _, ready in state)
            following = []
            for (key, part), (copies, _) in zip(parts, state):
                total = add_stage(key, part, stage, copies)
                ref[f"out{key}{stage}"][...] = total.astype(BF16)
                following.append(send_stage(key, part, stage + 1, ref[f"out{key}{stage}"]))
                ref[f"sum{key[:-1]}{stage}"][...] = total
            spend(0)
            state = following
        yield max(ready for _, ready in state)
        following = []
        for (key, part), (copies, _) in zip(parts, state):
            total = add_stage(key, part, final, copies).reshape(share, part[2])
            block = own_block(key[:-1], total, slice(part[1], part[1] + part[2]))
            ref[f"all{key}"][block_of(axes)] = block.reshape((1,) * len(dims) + (share, part[2]))
            following.append(gather_stage(key, part, final))
        spend(0)
        state = following
        for stage in reversed(range(final)):
            yield max(ready for _, ready in state)
            following = []
            for (key, part), (copies, _) in zip(parts, state):
                for copy in copies:
                    copy.wait_recv()
                following.append(gather_stage(key, part, stage))
            state = following
        yield max(ready for _, ready in state)
        for copies, _ in state:
            for copy in copies:
                copy.wait_recv()

    def gathered(b, pair, phase):
        sides = [
            ref[f"all{b}_{pair}{side}{phase}"][...].reshape(rows, part[2]) for side, part in enumerate(cuts[pair])
        ]
        return jnp.concatenate(sides, axis=1)

    def split():
        loads["w_dec"].wait()

        def step(i, carry):
            at = pl.ds(pl.multiple_of(i * 64, 64), 64)
            value = ref["w_dec_v"][at, :]
            high = value.astype(BF16)
            ref["high"][at, :] = high
            ref["low"][at, :] = (value - high.astype(F32)).astype(BF16)
            return carry

        lax.fori_loop(0, latents // 64, step, 0)
        loads["w_enc"].wait()
        spend(1e9)

    alive = ref["alive"][...].astype(F32)

    def count_up(key):
        ended[key] = ended.get(key, 0) + 1
        return ended[key]

    def forward(b, pair):
        columns = columns_of(pair)
        span = columns.stop - columns.start
        if pair == 0:
            picked = ref["picked"][:, b].reshape(rows, count * batches * share)
            chosen = lax.dot_general(picked, ref["hidden_v"][...], last, preferred_element_type=F32)
            ref[f"chosen{b}"][...] = chosen.astype(BF16)
            spend(2 * rows * depth * count * batches * share)
        lhs = ref[f"chosen{b}"][...]
        value = jnp.dot(lhs, ref["w_down_v"][:, columns], preferred_element_type=F32)
        spend(2 * rows * depth * span)
        yield from exchange(b, pair, 0, value, lambda key, total, columns: total.astype(BF16))
        if not ended:
            split()
        term = jnp.dot(gathered(b, pair, 0), ref["w_enc_v"][columns, :], preferred_element_type=F32)
        spend(2 * rows * latents * span)
        encoded = ref[f"encoded{b}"]
        number = count_up((b, 0))
        encoded[...] = term if number == 1 else encoded[...] + term
        if number < pairs:
            return
        copies = [send(encoded, ref[f"encoded_in{b}"].at[s - 1], layer_peer(s)[1]) for s in range(1, layers)]
        yield busy("layer", rows * latents * 4 * (layers - 1), LOCAL)
        for copy in copies:
            copy.wait_recv()
        preact = encoded[...]
        for s in range(layers - 1):
            preact = preact + ref[f"encoded_in{b}"][s]
        preact = preact + ref["b_enc"][...]
        latent = (jnp.maximum(preact, 0.0) * alive).astype(BF16)
        ref[f"latent{b}"][...] = latent.reshape(count, share, latents)
        ref["latent_out"][:, b] = ref[f"latent{b}"][pl.ds(layer * per_layer, per_layer)]
        spend(0)
        waiting.extend(backward(b, later) for later in range(pairs))

    def backward(b, pair):
        left = ref[f"latent{b}"][...].reshape(rows, latents)
        columns = columns_of(pair)
        span = columns.stop - columns.start
        value = jnp.dot(left, ref["high"][:, columns], preferred_element_type=F32)
        value = value + jnp.dot(left, ref["low"][:, columns], preferred_element_type=F32)
        spend(4 * rows * latents * span)

        def residual_block(key, total, columns):
            own = ref[f"all{key}0"][block_of(axes)].reshape(total.shape).astype(F32)
            residual = own - (total + ref["b_dec"][:, columns])
            ref["residual_out"][b, :, columns] = residual
            return residual.astype(BF16)

        yield from exchange(b, pair, 1, value, residual_block)
        wide = gathered(b, pair, 1)
        term = lax.dot_general(wide, ref["high"][:, columns], last, preferred_element_type=F32)
        term = term + lax.dot_general(wide, ref["low"][:, columns], last, preferred_element_type=F32)
        term = term.reshape(count, share, latents)
        spend(4 * rows * latents * span)
        back = ref[f"back{b}"]
        number = count_up((b, 1))
        back[...] = term if number == 1 else back[...] + term
        if number < pairs:
            return
        copies = []
        for s in range(1, layers):
            other, device = layer_peer(s)
            block = back.at[pl.ds(other * per_layer, per_layer)]
            copies.append(send(block, ref[f"back_in{b}"].at[s - 1], device))
        yield busy("layer", rows * latents * 4 * (layers - 1) // layers, LOCAL)
        for copy in copies:
            copy.wait_recv()
        total = back[pl.ds(layer * per_layer, per_layer)]
        for s in range(layers - 1):
            total = total + ref[f"back_in{b}"][s]
        ref["adjoint_out"][:, b] = -total * alive[None]
        spend(0)

    waiting.extend(forward(b, pair) for b in range(batches) for pair in range(pairs))
    while active or waiting:
        active.sort(key=lambda entry: entry[0])
        if waiting and (not active or max(free[orders[0][0]], free[orders[1][0]]) <= max(active[0][0], clock[0]) + SLACK):
            item = waiting.pop(0)
        else:
            ready, _, item = active.pop(0)
            clock[0] = max(clock[0], ready)
        ready = next(item, None)
        if ready is not None:
            active.append((ready, len(active), item))
    for copy in sent:
        copy.wait_send()


def copy_kernel(*refs):
    for source, target in zip(refs[:3], refs[3:]):
        target[...] = source[...]


def per_device(dims, layers, hidden, row_list, w_down, w_enc, b_enc, w_dec, b_dec, alive_mask):
    count = math.prod(dims)
    hidden = jnp.swapaxes(hidden, 1, 2)
    _, depth, row_count = hidden.shape
    width, latents = w_enc.shape[1:]
    cuts, orders = cuts_of(width), orders_of(dims)
    batches = 2 if row_count // count % 32 == 0 else 1
    share = row_count // count // batches
    rows = count * share

    scratch = {
        "hidden_v": pltpu.VMEM((depth, row_count), BF16),
        "w_down_v": pltpu.VMEM((depth, width), BF16),
        "w_enc_v": pltpu.VMEM((width, latents), BF16),
        "w_dec_v": pltpu.VMEM((latents, width), F32),
        "high": pltpu.VMEM((latents, width), BF16),
        "low": pltpu.VMEM((latents, width), BF16),
        "picked": pltpu.VMEM((count, batches, share, row_count), BF16),
    }
    for b in range(batches):
        scratch[f"chosen{b}"] = pltpu.VMEM((rows, depth), BF16)
        scratch[f"encoded{b}"] = pltpu.VMEM((rows, latents), F32)
        scratch[f"encoded_in{b}"] = pltpu.VMEM((max(layers - 1, 1), rows, latents), F32)
        scratch[f"latent{b}"] = pltpu.VMEM((count, share, latents), BF16)
        scratch[f"back{b}"] = pltpu.VMEM((count, share, latents), F32)
        scratch[f"back_in{b}"] = pltpu.VMEM((max(layers - 1, 1), count // layers, share, latents), F32)
        for pair, side in [(pair, side) for pair, parts in enumerate(cuts) for side in range(len(parts))]:
            key = f"{b}_{pair}{side}"
            kind, _, part = cuts[pair][side]
            scratch[f"wide{key}"] = pltpu.VMEM(dims + (share, part), F32)
            for phase in range(2):
                scratch[f"narrow{key}{phase}"] = pltpu.VMEM(dims + (share, part), BF16)
                scratch[f"all{key}{phase}"] = pltpu.VMEM(dims + (share, part), BF16)
            left = list(dims)
            for stage, axis in enumerate(orders[kind]):
                left[axis] = 1
                for phase in range(2):
                    shape = (max(dims[axis] - 1, 1), *left, share, part)
                    scratch[f"in{key}{phase}{stage}"] = pltpu.VMEM(shape, BF16)
                    if stage < len(dims) - 1:
                        scratch[f"out{key}{phase}{stage}"] = pltpu.VMEM((*left, share, part), BF16)
                if stage < len(dims) - 1:
                    scratch[f"sum{key}{stage}"] = pltpu.VMEM((*left, share, part), F32)
    copies = 4 * batches * sum(map(len, cuts)) * sum(d - 1 for d in dims) + 2 * batches * (layers - 1)
    scratch["load"] = pltpu.SemaphoreType.DMA((4,))
    scratch["send"] = pltpu.SemaphoreType.DMA((copies,))
    scratch["recv"] = pltpu.SemaphoreType.DMA((copies,))

    names = ("hidden", "w_down", "w_enc", "w_dec", "row_list", "b_enc", "b_dec", "alive")
    names += ("latent_out", "residual_out", "adjoint_out") + tuple(scratch)
    vmem = pl.BlockSpec(memory_space=pltpu.VMEM)
    hbm = pl.BlockSpec(memory_space=pl.ANY)
    own = (count // layers, batches, share, latents)
    latent, residual, adjoint = pl.pallas_call(
        functools.partial(kernel, dims, cuts, layers, batches, share, depth, width, latents, names),
        out_shape=(
            jax.ShapeDtypeStruct(own, BF16),
            jax.ShapeDtypeStruct((batches, share, width), F32),
            jax.ShapeDtypeStruct(own, F32),
        ),
        in_specs=[hbm] * 4 + [vmem] * 4,
        out_specs=(vmem, vmem, vmem),
        scratch_shapes=list(scratch.values()),
        compiler_params=pltpu.CompilerParams(
            collective_id=0, has_side_effects=True, vmem_limit_bytes=62 * 1024 * 1024
        ),
    )(hidden, w_down, w_enc, w_dec, row_list[None], b_enc[None], b_dec, alive_mask[None])
    results = (latent.reshape(-1, latents), residual.reshape(1, -1, width), adjoint.reshape(-1, latents))
    return tuple(
        pl.pallas_call(
            copy_kernel,
            out_shape=tuple(jax.ShapeDtypeStruct(a.shape, a.dtype) for a in results),
            in_specs=[vmem] * 3,
            out_specs=(vmem,) * 3,
        )(*results)
    )


def solution(mesh):
    return jax.shard_map(
        functools.partial(per_device, digits_of(mesh), mesh.shape["layer"]),
        mesh=mesh,
        in_specs=(
            P("layer", None, "dict"),
            P(),
            P("layer", "dict", None),
            P("layer", None, "dict"),
            P("dict"),
            P("layer", "dict", None),
            P("layer", None),
            P("dict"),
        ),
        out_specs=(P("layer", "dict"), P("layer", "dict", None), P("layer", "dict")),
        check_vma=False,
    )
```

time: 141 us -> 102 us (0.72)
  Pallas kernels: 140 us -> 101 us
    pallas_call x1, Pallas kernels: 33.9 us -> 2.21 us  [per_device(): pl.pallas_call(copy_kernel, out_shape=tuple((jax.ShapeDtypeStruct(a.shape...]
    pallas_call x1, Pallas kernels: 106 us -> 99 us  [per_device(): pl.pallas_call(functools.partial(kernel, dims, cuts, layers, batches, sha...]
where the time goes in v3:
time: 102 us
  Pallas kernels  101 us (99%)
    pallas_call x1, Pallas kernels, per_device(): pl.pallas_call(functools.partial(kernel, dims, cuts, layers, batches, sha...  99 us
    pallas_call x1, Pallas kernels, per_device(): pl.pallas_call(copy_kernel, out_shape=tuple((jax.ShapeDtypeStruct(a.shape...  2.21 us

profile of v3, /device:TPU:1, one launch (start us, length us, event | category | flops | bytes accessed | tf_op | source)
XLA Modules:
  0.0 101.8 jit_solution(6704609856401592745)
XLA Ops:
  0.6 99.0 %shard_map.103 = (bf16[8,2,16,512]{3,2,1,0:T(8,128)(2,1)}, f32[2,16,2304]{2,1,0:T(8,128)}, f32[8,2,16,512]{3,2,1,0:T(8,128)}) custom-call(bf16[1,576,512]{2,1,0:T(8,128)(2,1)} %bitcast.7, bf16[1,576,2304]{2,1,0:T(8,128)(2,1)} %refs_1_.1, bf16[1,2304,512]{2,1,0:T(8,128)(2,1)} %refs_2_.1, f32[1,512,2304]{2,1,0:T(8,128)} %refs_3_.1, s32[1,512]{1,0:T(1,128)} %bitcast.11, ...), custom_call_target="tpu_custom_call" | custom-call | tf_op jit(solution)/shard_map/pallas_call | solution.py:383
  99.6 2.2 %shard_map.104 = (bf16[256,512]{1,0:T(8,128)(2,1)}, f32[1,32,2304]{2,1,0:T(8,128)}, f32[256,512]{1,0:T(8,128)}) custom-call(bf16[256,512]{1,0:T(8,128)(2,1)} %bitcast.10, f32[1,32,2304]{2,1,0:T(8,128)} %bitcast.9, f32[256,512]{1,0:T(8,128)} %bitcast.8), custom_call_target="tpu_custom_call" | custom-call | tf_op jit(solution)/shard_map/pallas_call | solution.py:399

commit v4 on v3

--- a/solution.py
+++ b/solution.py
@@ -123,8 +123,13 @@
     loads["w_dec"].start()
     pl.semaphore_wait(barrier, len(peers))
 
-    def block_of(among):
-        return tuple(pl.ds(mine[a], 1) if a in among else slice(None) for a in axes)
+    def block_of(kind, stages):
+        return tuple(pl.ds(mine[a], 1) if i in stages else slice(None) for i, a in enumerate(orders[kind]))
+
+    def places(kind):
+        return [
+            tuple(block // strides[a] % dims[a] for a in orders[kind]) for block in range(count)
+        ]
 
     def stage_cost(axis, blocks, columns):
         length = 2 * blocks * share * columns * 2
@@ -139,7 +144,7 @@
         copies = []
         for step in range(1, dims[axis]):
             other, device = peer_of(axis, step)
-            index = tuple(pl.ds(other, 1) if a == axis else slice(None) for a in axes)
+            index = tuple(pl.ds(other, 1) if i == stage else slice(None) for i in axes)
             copies.append(send(source.at[index], ref[f"in{key}{stage}"].at[step - 1], device))
         left = math.prod(dims[a] for a in orders[kind][stage + 1 :])
         return copies, stage_cost(axis, left, columns)
@@ -149,14 +154,14 @@
         own = ref[f"wide{key[:-1]}"] if stage == 0 else ref[f"sum{key[:-1]}{stage - 1}"]
         for copy in copies:
             copy.wait_recv()
-        total = own[block_of((axis,))]
+        total = own[block_of(part[0], (stage,))]
         for step in range(dims[axis] - 1):
             total = total + ref[f"in{key}{stage}"][step].astype(F32)
         return total
 
     def gather_stage(key, part, stage):
         kind, _, columns = part
-        block = ref[f"all{key}"].at[block_of(orders[kind][: stage + 1])]
+        block = ref[f"all{key}"].at[block_of(kind, range(stage + 1))]
         axis = orders[kind][stage]
         copies = [send(block, block, peer_of(axis, step)[1]) for step in range(1, dims[axis])]
         left = math.prod(dims[a] for a in orders[kind][stage + 1 :])
@@ -170,9 +175,10 @@
         state, final = [], len(dims) - 1
         for key, part in parts:
             start = part[1] - cuts[pair][0][1]
-            term = value[:, start : start + part[2]].reshape(dims + (share, part[2]))
-            ref[f"wide{key[:-1]}"][...] = term
-            ref[f"narrow{key}"][...] = term.astype(BF16)
+            for block, at in enumerate(places(part[0])):
+                term = value[block * share : (block + 1) * share, start : start + part[2]]
+                ref[f"wide{key[:-1]}"][at] = term
+                ref[f"narrow{key}"][at] = term.astype(BF16)
             state.append(send_stage(key, part, 0, ref[f"narrow{key}"]))
         for stage in range(final):
             yield max(ready for _, ready in state)
@@ -188,8 +194,9 @@
         following = []
         for (key, part), (copies, _) in zip(parts, state):
             total = add_stage(key, part, final, copies).reshape(share, part[2])
-            block = own_block(key[:-1], total, slice(part[1], part[1] + part[2]))
-            ref[f"all{key}"][block_of(axes)] = block.reshape((1,) * len(dims) + (share, part[2]))
+            index = block_of(part[0], axes)
+            block = own_block(key[:-1], index, total, slice(part[1], part[1] + part[2]))
+            ref[f"all{key}"][index] = block.reshape((1,) * len(dims) + (share, part[2]))
             following.append(gather_stage(key, part, final))
         spend(0)
         state = following
@@ -208,7 +215,8 @@
 
     def gathered(b, pair, phase):
         sides = [
-            ref[f"all{b}_{pair}{side}{phase}"][...].reshape(rows, part[2]) for side, part in enumerate(cuts[pair])
+            jnp.concatenate([ref[f"all{b}_{pair}{side}{phase}"][at] for at in places(part[0])], axis=0)
+            for side, part in enumerate(cuts[pair])
         ]
         return jnp.concatenate(sides, axis=1)
 
@@ -244,7 +252,7 @@
         lhs = ref[f"chosen{b}"][...]
         value = jnp.dot(lhs, ref["w_down_v"][:, columns], preferred_element_type=F32)
         spend(2 * rows * depth * span)
-        yield from exchange(b, pair, 0, value, lambda key, total, columns: total.astype(BF16))
+        yield from exchange(b, pair, 0, value, lambda key, index, total, columns: total.astype(BF16))
         if not ended:
             split()
         term = jnp.dot(gathered(b, pair, 0), ref["w_enc_v"][columns, :], preferred_element_type=F32)
@@ -266,7 +274,7 @@
         ref[f"latent{b}"][...] = latent.reshape(count, share, latents)
         ref["latent_out"][:, b] = ref[f"latent{b}"][pl.ds(layer * per_layer, per_layer)]
         spend(0)
-        waiting.extend(backward(b, later) for later in range(pairs))
+        waiting.extend((later, backward(b, later)) for later in range(pairs))
 
     def backward(b, pair):
         left = ref[f"latent{b}"][...].reshape(rows, latents)
@@ -276,8 +284,8 @@
         value = value + jnp.dot(left, ref["low"][:, columns], preferred_element_type=F32)
         spend(4 * rows * latents * span)
 
-        def residual_block(key, total, columns):
-            own = ref[f"all{key}0"][block_of(axes)].reshape(total.shape).astype(F32)
+        def residual_block(key, index, total, columns):
+            own = ref[f"all{key}0"][index].reshape(total.shape).astype(F32)
             residual = own - (total + ref["b_dec"][:, columns])
             ref["residual_out"][b, :, columns] = residual
             return residual.astype(BF16)
@@ -307,11 +315,17 @@
         ref["adjoint_out"][:, b] = -total * alive[None]
         spend(0)
 
-    waiting.extend(forward(b, pair) for b in range(batches) for pair in range(pairs))
+    def links_free(pair):
+        return max(free[orders[kind][0]] for kind, _, _ in cuts[pair])
+
+    waiting.extend((pair, forward(b, pair)) for b in range(batches) for pair in range(pairs))
     while active or waiting:
         active.sort(key=lambda entry: entry[0])
-        if waiting and (not active or max(free[orders[0][0]], free[orders[1][0]]) <= max(active[0][0], clock[0]) + SLACK):
-            item = waiting.pop(0)
+        until = max(active[0][0], clock[0]) + SLACK if active else math.inf
+        start = next((entry for entry in waiting if links_free(entry[0]) <= until), None)
+        if start:
+            waiting.remove(start)
+            item = start[1]
         else:
             ready, _, item = active.pop(0)
             clock[0] = max(clock[0], ready)
@@ -356,13 +370,13 @@
         for pair, side in [(pair, side) for pair, parts in enumerate(cuts) for side in range(len(parts))]:
             key = f"{b}_{pair}{side}"
             kind, _, part = cuts[pair][side]
-            scratch[f"wide{key}"] = pltpu.VMEM(dims + (share, part), F32)
+            left = [dims[axis] for axis in orders[kind]]
+            scratch[f"wide{key}"] = pltpu.VMEM((*left, share, part), F32)
             for phase in range(2):
-                scratch[f"narrow{key}{phase}"] = pltpu.VMEM(dims + (share, part), BF16)
-                scratch[f"all{key}{phase}"] = pltpu.VMEM(dims + (share, part), BF16)
-            left = list(dims)
+                scratch[f"narrow{key}{phase}"] = pltpu.VMEM((*left, share, part), BF16)
+                scratch[f"all{key}{phase}"] = pltpu.VMEM((*left, share, part), BF16)
             for stage, axis in enumerate(orders[kind]):
-                left[axis] = 1
+                left[stage] = 1
                 for phase in range(2):
                     shape = (max(dims[axis] - 1, 1), *left, share, part)
                     scratch[f"in{key}{phase}{stage}"] = pltpu.VMEM(shape, BF16)

time: 102 us -> 102 us (level)
  no operation moved by 1% of the time
where the time goes in v4:
time: 102 us
  Pallas kernels  101 us (99%)
    pallas_call x1, Pallas kernels, per_device(): pl.pallas_call(functools.partial(kernel, dims, cuts, layers, batches, sha...  99 us
    pallas_call x1, Pallas kernels, per_device(): pl.pallas_call(copy_kernel, out_shape=tuple((jax.ShapeDtypeStruct(a.shape...  2.21 us

profile of v4, /device:TPU:1, one launch (start us, length us, event | category | flops | bytes accessed | tf_op | source)
XLA Modules:
  0.0 101.8 jit_solution(9063720759906036661)
XLA Ops:
  0.6 99.0 %shard_map.103 = (bf16[8,2,16,512]{3,2,1,0:T(8,128)(2,1)}, f32[2,16,2304]{2,1,0:T(8,128)}, f32[8,2,16,512]{3,2,1,0:T(8,128)}) custom-call(bf16[1,576,512]{2,1,0:T(8,128)(2,1)} %bitcast.7, bf16[1,576,2304]{2,1,0:T(8,128)(2,1)} %refs_1_.1, bf16[1,2304,512]{2,1,0:T(8,128)(2,1)} %refs_2_.1, f32[1,512,2304]{2,1,0:T(8,128)} %refs_3_.1, s32[1,512]{1,0:T(1,128)} %bitcast.11, ...), custom_call_target="tpu_custom_call" | custom-call | tf_op jit(solution)/shard_map/pallas_call | solution.py:397
  99.6 2.2 %shard_map.104 = (bf16[256,512]{1,0:T(8,128)(2,1)}, f32[1,32,2304]{2,1,0:T(8,128)}, f32[256,512]{1,0:T(8,128)}) custom-call(bf16[256,512]{1,0:T(8,128)(2,1)} %bitcast.10, f32[1,32,2304]{2,1,0:T(8,128)} %bitcast.9, f32[256,512]{1,0:T(8,128)} %bitcast.8), custom_call_target="tpu_custom_call" | custom-call | tf_op jit(solution)/shard_map/pallas_call | solution.py:413

commit v5 on v4

--- a/solution.py
+++ b/solution.py
@@ -45,11 +45,11 @@
 
 
 def cuts_of(width):
-    if width % 768 or width < 2304:
+    if width % 2304:
         return (((0, 0, width),),)
+    three, two, short = ((2, 256), (0, 256), (1, 256)), ((0, 256), (1, 256)), ((0, 128), (1, 128))
     groups, start = [], 0
-    for group in range(width // 768):
-        kinds = ((2, 256), (0, 256), (1, 256)) if group % 3 < 2 else ((0, 384), (1, 384))
+    for kinds in (three, two, three, short) * (width // 2304):
         parts = []
         for kind, columns in kinds:
             parts.append((kind, start, columns))
@@ -252,9 +252,12 @@
         lhs = ref[f"chosen{b}"][...]
         value = jnp.dot(lhs, ref["w_down_v"][:, columns], preferred_element_type=F32)
         spend(2 * rows * depth * span)
-        yield from exchange(b, pair, 0, value, lambda key, index, total, columns: total.astype(BF16))
-        if not ended:
+        steps = exchange(b, pair, 0, value, lambda key, index, total, columns: total.astype(BF16))
+        first = next(steps)
+        if b == 0 and pair == min(1, pairs - 1):
             split()
+        yield first
+        yield from steps
         term = jnp.dot(gathered(b, pair, 0), ref["w_enc_v"][columns, :], preferred_element_type=F32)
         spend(2 * rows * latents * span)
         encoded = ref[f"encoded{b}"]

time: 102 us -> 104 us (1.020)
  Pallas kernels: 101 us -> 103 us
    pallas_call x1, Pallas kernels: 99 us -> 101 us  [per_device(): pl.pallas_call(functools.partial(kernel, dims, cuts, layers, batches, sha...]
where the time goes in v5:
time: 104 us
  Pallas kernels  103 us (99%)
    pallas_call x1, Pallas kernels, per_device(): pl.pallas_call(functools.partial(kernel, dims, cuts, layers, batches, sha...  101 us
    pallas_call x1, Pallas kernels, per_device(): pl.pallas_call(copy_kernel, out_shape=tuple((jax.ShapeDtypeStruct(a.shape...  2.21 us

profile of v5, /device:TPU:1, one launch (start us, length us, event | category | flops | bytes accessed | tf_op | source)
XLA Modules:
  0.0 103.5 jit_solution(7476713768997490457)
XLA Ops:
  0.6 100.7 %shard_map.103 = (bf16[8,2,16,512]{3,2,1,0:T(8,128)(2,1)}, f32[2,16,2304]{2,1,0:T(8,128)}, f32[8,2,16,512]{3,2,1,0:T(8,128)}) custom-call(bf16[1,576,512]{2,1,0:T(8,128)(2,1)} %bitcast.7, bf16[1,576,2304]{2,1,0:T(8,128)(2,1)} %refs_1_.1, bf16[1,2304,512]{2,1,0:T(8,128)(2,1)} %refs_2_.1, f32[1,512,2304]{2,1,0:T(8,128)} %refs_3_.1, s32[1,512]{1,0:T(1,128)} %bitcast.11, ...), custom_call_target="tpu_custom_call" | custom-call | tf_op jit(solution)/shard_map/pallas_call | solution.py:400
  101.3 2.2 %shard_map.104 = (bf16[256,512]{1,0:T(8,128)(2,1)}, f32[1,32,2304]{2,1,0:T(8,128)}, f32[256,512]{1,0:T(8,128)}) custom-call(bf16[256,512]{1,0:T(8,128)(2,1)} %bitcast.10, f32[1,32,2304]{2,1,0:T(8,128)} %bitcast.9, f32[256,512]{1,0:T(8,128)} %bitcast.8), custom_call_target="tpu_custom_call" | custom-call | tf_op jit(solution)/shard_map/pallas_call | solution.py:416
